TPU v7x, 128 devices: a whole 4x4x4 slice. The times are simulated.
128 devices in a mesh: frame: 8 (over z, y_hi), token: 8 (over x, y_lo), batch: 2 (over core).
Axes of the slice: x: 4, y: 4 (y_hi: 2, y_lo: 2; y = y_hi * 2 + y_lo), z: 4, core: 2. Of those that a mesh axis runs over, the one named last changes fastest.
Arguments:
- encoder_out: bfloat16 [2, 512, 512], P('batch', 'frame', 'token'), may hold values from -6 to 6
- predictor_out: bfloat16 [2, 512, 512], P('batch', 'token', 'frame'), may hold values from -6 to 6
- enc_weight: bfloat16 [512, 512], replicated, may hold values from -0.25 to 0.25
- pred_weight: bfloat16 [512, 512], replicated, may hold values from -0.25 to 0.25
- joint_bias: float32 [512], replicated, may hold values from -0.5 to 0.5
- out_weight: bfloat16 [512, 1024], replicated, may hold values from -0.076171875 to 0.076171875
- blank_occupancy: float32 [2, 512, 512], P('batch', 'frame', 'token'), may hold values from 0.05 to 1
- label_occupancy: float32 [2, 512, 512], P('batch', 'frame', 'token'), may hold values from 0.05 to 1
- frame_lengths: int32 [2], replicated, may hold values from 64 to 512, as said below
- token_lengths: int32 [2], replicated, may hold values from 64 to 511, as said below
- target_ids: int32 [2, 512], P(None, 'token'), may hold values from 1 to 1023
Outputs:
- enc_grad: float32 [2, 512, 512], P('batch', 'frame', 'token')
- pred_grad: float32 [2, 512, 512], P('batch', 'token', 'frame')
- enc_weight_grad: float32 [512, 512], P(('frame', 'token', 'batch'))
- pred_weight_grad: float32 [512, 512], P(('frame', 'token', 'batch'))
- out_weight_grad: float32 [512, 1024], P(('frame', 'token', 'batch'))
- bias_grad: float32 [512], P(('frame', 'token', 'batch'))
Inputs may be any that keep to these rules, and one draw needn't show every extreme that they name: `frame_lengths`: frames of each utterance; in every draw some utterance has all 512. `token_lengths`: target tokens of each utterance; in every draw some utterance has 511. `target_ids`: entry 0 is the blank and is never a target.
All inputs are finite; a program needn't handle non-finite values.
Results may differ from a plain program's by a relative error of at most 0.00059.
Values may be sent and summed in bfloat16 or wider, within the bound.
No kernel may reach another device: no remote copies, remote signals or barrier semaphores. Data moves between devices by JAX's collectives and lax.ppermute only.
A program may use at most 64 MiB of HBM per device.

v0:
```python
import jax
import jax.numpy as jnp
from jax import lax
from jax.experimental import pallas as pl
from jax.experimental.pallas import tpu as pltpu
from jax.sharding import PartitionSpec as P

FB = 16
CHUNK = 256
LEVELS = 32000.0
STEPS = 16.0
SMALL = 8
TAIL = 16
ALL = ("frame", "token", "batch")
F32, BF16 = jnp.float32, jnp.bfloat16


def split3(x):
    hi = x.astype(BF16)
    rest = x - hi.astype(F32)
    mid = rest.astype(BF16)
    lo = (rest - mid.astype(F32)).astype(BF16)
    return hi, mid, lo


def dot_nt(a, b):
    return lax.dot_general(a, b, (((1,), (1,)), ((), ())), preferred_element_type=F32)


def dot_tn(a, b):
    return lax.dot_general(a, b, (((0,), (0,)), ((), ())), preferred_element_type=F32)


def exact_nt(a, b):
    rows = a.shape[0]
    product = dot_nt(jnp.concatenate(split3(a), axis=0), b)
    return product[:rows] + product[rows : 2 * rows] + product[2 * rows :]


def to_levels(x):
    largest = jnp.maximum(jnp.max(jnp.abs(x), axis=-1, keepdims=True), 1e-30)
    power = jnp.ceil(jnp.log2(largest) * STEPS)
    return jnp.round(x * (LEVELS * jnp.exp2(power * (-1.0 / STEPS)))), power


def from_levels(x, powers):
    rows = x.shape[0]
    diag = lax.broadcasted_iota(jnp.int32, (rows, 128), 0) == lax.broadcasted_iota(jnp.int32, (rows, 128), 1)
    power = jnp.sum(jnp.where(diag, powers, 0.0), axis=1, keepdims=True)
    return x * (jnp.exp2(power * (1.0 / STEPS)) * (1.0 / LEVELS))


def halves(ref, first_half):
    width = ref.shape[2] // 2
    start = 0 if first_half else width
    pieces = [ref[s].astype(F32)[:, start : start + width] for s in range(ref.shape[0])]
    return jnp.concatenate(pieces, axis=1).astype(BF16)


def exact_tn(a, b):
    return sum(dot_tn(a, piece) for piece in split3(b))


def cells_kernel(
    g_ref, h_ref, weights_ref, cell_ref, keep_ref, send_ref, ow_keep_ref, ow_send_ref, feat_ref,
    encp_ref, predp_ref, rows_ref, prow_ref, tgt_col_ref, occ_ref, e_ref, stash_ref,
):
    nf, nt = encp_ref.shape[0], predp_ref.shape[0]
    joint, vocab = encp_ref.shape[1], e_ref.shape[1]
    ow_ref = weights_ref.at[:, :vocab]
    encw_ref = weights_ref.at[:, vocab : vocab + joint]
    predw_ref = weights_ref.at[:, vocab + joint :]
    parts, width = g_ref.shape[0], g_ref.shape[2] // 2
    cells = FB * nt
    first = lax.axis_index("batch") == 0
    own, other = halves(g_ref, True), halves(h_ref, False)
    feat_ref[...] = jnp.concatenate([own.astype(F32).T, halves(g_ref, False).astype(F32).T], axis=1).astype(BF16)
    encp_ref[...] = jnp.dot(jnp.where(first, own, other), encw_ref[...], preferred_element_type=F32)
    predp = jnp.dot(jnp.where(first, other, own), predw_ref[...], preferred_element_type=F32)
    for v in range(joint // 128):
        cols = slice(v * 128, (v + 1) * 128)
        predp_ref[:, cols] = predp[:, cols] + cell_ref[nf + v : nf + v + 1, :]
    diag_row = lax.broadcasted_iota(jnp.int32, (nt, 128), 0)
    diag_lane = lax.broadcasted_iota(jnp.int32, (nt, 128), 1)
    blank_diag, label_diag = diag_row == diag_lane, diag_row + nt == diag_lane
    core = lax.axis_index("batch")
    row = nf + joint // 128
    mine = diag_row + nt * core == diag_lane
    targets = jnp.sum(jnp.where(mine, cell_ref[row : row + 1, :], 0.0), axis=1, keepdims=True)
    tgt_col_ref[...] = jnp.broadcast_to(targets.astype(jnp.int32), (nt, 128))
    lengths = cell_ref[row + 1 : row + 2, :]
    lane1 = diag_lane[:1]
    frame_len = jnp.sum(jnp.where(lane1 == core, lengths, 0.0), axis=1, keepdims=True).astype(jnp.int32)
    token_len = jnp.sum(jnp.where(lane1 == core + 2, lengths, 0.0), axis=1, keepdims=True).astype(jnp.int32)
    frame_pos = lax.axis_index("frame") * nf + lax.broadcasted_iota(jnp.int32, (nf, 128), 0)
    token_pos = lax.axis_index("token") * nt + lax.rem(lax.broadcasted_iota(jnp.int32, (nf, 128), 1), nt)
    reach = jnp.where(lax.broadcasted_iota(jnp.int32, (nf, 128), 1) < nt, token_len, token_len - 1)
    occ_ref[...] = jnp.where((frame_pos < frame_len) & (token_pos <= reach), cell_ref[:nf, :], 0.0)
    prow_ref[...] = jnp.zeros_like(prow_ref)
    lane = lax.broadcasted_iota(jnp.int32, (FB, nt, 128), 2)

    def columns(diag, t0):
        rows = occ_ref[pl.ds(t0, FB), :]
        return jnp.sum(jnp.where(diag[None], rows[:, None, :], 0.0), axis=2, keepdims=True)

    def block(i, carry):
        t0 = pl.multiple_of(i * FB, FB)
        span = pl.ds(pl.multiple_of(i * cells, cells), cells)
        frames = encp_ref[pl.ds(t0, FB), :]
        inner = frames[:, None, :] + predp_ref[...][None, :, :]
        hidden = jnp.tanh(inner).astype(BF16).reshape(cells, joint)
        stash_ref[span, :joint] = hidden
        total = jnp.zeros((cells, 128), F32)
        for c in range(vocab // CHUNK):
            cols = slice(c * CHUNK, (c + 1) * CHUNK)
            e = jnp.exp(jnp.dot(hidden, ow_ref[:, cols], preferred_element_type=F32))
            e_ref[:, cols] = e
            for q in range(CHUNK // 128):
                total = total + e[:, q * 128 : (q + 1) * 128]
        total = jnp.sum(total, axis=1, keepdims=True).reshape(FB, nt, 1)
        bw = columns(blank_diag, t0)
        lw = columns(label_diag, t0)
        scale = (bw + lw) / total
        tgt = tgt_col_ref[...][None]
        for v in range(vocab // 128):
            cols = slice(v * 128, (v + 1) * 128)
            g = e_ref[:, cols].reshape(FB, nt, 128) * scale
            if v == 0:
                g = g - jnp.where(lane == 0, bw, 0.0)
            g = g - jnp.where(lane == tgt - v * 128, lw, 0.0)
            stash_ref[span, joint + v * 128 : joint + (v + 1) * 128] = g.astype(BF16).reshape(cells, 128)
        for c in range(joint // CHUNK):
            cols = slice(c * CHUNK, (c + 1) * CHUNK)
            grad_hidden = dot_nt(stash_ref[span, joint:], ow_ref[cols, :])
            hf = stash_ref[span, cols].astype(F32)
            gi = (grad_hidden * (1.0 - hf * hf)).reshape(FB, nt, CHUNK)
            prow_ref[:, cols] += gi.sum(0)
            rows_ref[pl.ds(t0, FB), cols] = gi.sum(1)
        return carry

    lax.fori_loop(0, nf // FB, block, 0)

    term_e = exact_nt(rows_ref[...], encw_ref[...])
    term_p = exact_nt(prow_ref[...], predw_ref[...])
    for s in range(parts):
        cols = slice(s * width, (s + 1) * width)
        e_part = jnp.concatenate([term_e[:, cols], rows_ref[:, cols]], axis=1)
        p_part = jnp.concatenate([term_p[:, cols], prow_ref[:, cols]], axis=1)
        for ref, part in ((keep_ref, jnp.where(first, e_part, p_part)), (send_ref, jnp.where(first, p_part, e_part))):
            q, power = to_levels(part)
            powers = jnp.sum(jnp.where(blank_diag, power, 0.0), axis=0, keepdims=True)
            q = jnp.concatenate([q, jnp.broadcast_to(powers, (TAIL, 128))], axis=0)
            ref[s, : nt + TAIL, :] = q.astype(jnp.int32).astype(jnp.int16)

    chips = joint // 8
    top = lax.broadcasted_iota(jnp.int32, (chips, 8, 128), 1) < 4
    half = vocab // 2
    for dest_ref, part in ((ow_send_ref, 1 - core), (ow_keep_ref, core)):
        start = pl.multiple_of(joint + part * half, 128)
        acc = dot_tn(stash_ref[:, :joint], stash_ref[:, pl.ds(start, half)])
        for v in range(half // 256):
            a = acc[:, v * 256 : v * 256 + 128].reshape(chips, 8, 128)
            b = acc[:, v * 256 + 128 : v * 256 + 256].reshape(chips, 8, 128)
            dest_ref[v, :, 0] = jnp.where(top, a, pltpu.roll(b, 4, 1))
            dest_ref[v, :, 1] = jnp.where(top, pltpu.roll(a, 4, 1), b)


def pack_kernel(keep_ref, recv_ref, y_ref, feat_ref, out_ref, total_ref, small_ref):
    tiles, chips = keep_ref.shape[:2]
    big = tiles * 8
    span = y_ref.shape[1] // 2
    nt = span - TAIL
    for h in range(2):
        total = jnp.zeros((nt, y_ref.shape[2]), F32)
        for s in range(y_ref.shape[0]):
            x = y_ref[s, h * span : (h + 1) * span, :].astype(jnp.int32).astype(F32)
            total = total + from_levels(x[:nt], x[nt : nt + 1])
        total_ref[h * nt : (h + 1) * nt, :] = total
    total = total_ref[...]
    width = total.shape[1] // 2
    rows_grad = total[:, width:]
    pieces = jnp.concatenate(split3(rows_grad), axis=1)
    product = jnp.dot(feat_ref[...], pieces, preferred_element_type=F32)
    weights = product[:, :width] + product[:, width : 2 * width] + product[:, 2 * width :]
    weights = jnp.concatenate([weights, jnp.zeros_like(weights)], axis=1).reshape(chips, SMALL, 2 * width)
    bias = jnp.sum(rows_grad, axis=0, keepdims=True)
    bias = jnp.concatenate([bias, jnp.zeros_like(bias)], axis=1)[None]
    sub = lax.broadcasted_iota(jnp.int32, weights.shape, 1)
    for c in range(2):
        own = weights if c == 0 else pltpu.roll(weights, 4, 1)
        small_ref[:, c] = jnp.where(sub < 4, own, jnp.where(sub == 4, bias, 0.0))

    batch = 16
    rows = big + SMALL
    row = lax.broadcasted_iota(jnp.int32, (batch, rows, 128), 1)
    diag = row == lax.broadcasted_iota(jnp.int32, (batch, rows, 128), 2)
    for i in range(0, chips, batch // 2):
        part = slice(i, i + batch // 2)
        parts = [keep_ref[v, part] + recv_ref[v, part] for v in range(tiles)] + [small_ref[part]]
        x = jnp.concatenate([p.reshape(batch, 8, 128) for p in parts], axis=1)
        q, power = to_levels(x)
        powers = jnp.sum(jnp.where(diag, power, 0.0), axis=1, keepdims=True)
        q = jnp.where(row == rows - 1, powers, q)
        out_ref[2 * i : 2 * i + batch] = q.astype(jnp.int32).astype(jnp.int16)


def last_kernel(z_ref, own_ref, partner_ref, enc_ref, pred_ref, encw_ref, predw_ref, outw_ref, bias_ref):
    core = lax.axis_index("batch")
    first = core == 0
    frame = lax.axis_index("frame")
    rows = z_ref.shape[1]
    big = rows - SMALL
    n = 8
    width = own_ref.shape[1] // 2
    total = [jnp.zeros((big, 128), F32)] * 2
    by_token = [jnp.zeros((SMALL, 128), F32)] * n
    by_frame = [jnp.zeros((SMALL, 128), F32)] * n
    for f in range(n):
        for k in range(n):
            for c in range(2):
                x = z_ref[(f * n + k) * 2 + c].astype(jnp.int32).astype(F32)
                x = from_levels(x, x[rows - 1 :])
                total[c] = total[c] + x[:big]
                if c == 0:
                    by_token[k] = by_token[k] + x[big:]
                else:
                    by_frame[f] = by_frame[f] + x[big:]
    for c in range(2):
        for t in range(big // 4):
            v = c * (big // 4) + t
            outw_ref[:, v * 128 : (v + 1) * 128] = total[c][t * 4 : t * 4 + 4, :]
    bias = jnp.zeros((1, 128), F32)
    for j in range(n):
        cols = slice(j * width, (j + 1) * width)
        encw_ref[:, cols] = by_token[j][:4, :width]
        predw_ref[:, cols] = by_frame[j][:4, :width]
        bias = bias + jnp.where(frame == j, by_token[j][4:5], 0.0)
    offset = lax.axis_index("token") * 8 + core * 4
    bias_ref[...] = pltpu.roll(bias, 128 - offset, 1)[:, :4]
    nt = enc_ref.shape[1]
    own, other = own_ref[:nt, :width], partner_ref[nt:, :width]
    enc_ref[0] = jnp.where(first, own, other)
    pred_ref[0] = jnp.where(first, other, own)


VM = pl.BlockSpec(memory_space=pltpu.VMEM)


def shape(*dims):
    return jax.ShapeDtypeStruct(dims, F32)


def local(
    encoder_out, predictor_out, enc_weight, pred_weight, joint_bias, out_weight,
    blank_occupancy, label_occupancy, frame_lengths, token_lengths, target_ids,
):
    joint, vocab = out_weight.shape
    nf, nt = blank_occupancy.shape[1:]
    width = encoder_out.shape[2]
    core = lax.axis_index("batch")
    n = lax.axis_size("frame")
    groups = [[f * 2 * n + k * 2 for k in range(n)] for f in range(n)]
    groups += [[f * 2 * n + k * 2 + 1 for f in range(n)] for k in range(n)]

    def swap(x):
        return lax.ppermute(x, "batch", [(0, 1), (1, 0)])

    def exchange(x):
        return lax.all_to_all(x, ALL, 0, 0, axis_index_groups=groups)

    enc, pred = encoder_out[0], predictor_out[0]
    def spread(own, other):
        return jnp.broadcast_to(jnp.where(core == 0, own, other)[None], (n, nf, width))

    payload = jnp.concatenate([spread(enc, pred), spread(swap(enc), swap(pred))], axis=2)
    (
        payload, enc_weight, pred_weight, out_weight, blank_occupancy, label_occupancy, joint_bias, target_ids,
        frame_lengths, token_lengths,
    ) = lax.optimization_barrier((
        payload, enc_weight, pred_weight, out_weight, blank_occupancy, label_occupancy, joint_bias, target_ids,
        frame_lengths, token_lengths,
    ))
    gathered = exchange(payload)

    cells = nf * nt
    lengths = jnp.concatenate([frame_lengths, token_lengths])
    per_cell = jnp.concatenate(
        [
            jnp.concatenate([blank_occupancy[0], label_occupancy[0]], axis=1),
            joint_bias.reshape(joint // 128, 128),
            target_ids.astype(F32).reshape(1, 2 * nt),
            jnp.pad(lengths.astype(F32)[None], ((0, 2), (0, 128 - lengths.shape[0]))),
        ],
        axis=0,
    )
    weights = jnp.concatenate([out_weight, enc_weight, pred_weight], axis=1)
    gathered, weights, per_cell = lax.optimization_barrier((gathered, weights, per_cell))
    partner = swap(gathered)
    tiles = vocab // 512
    term_keep, term_send, ow_keep, ow_send, features = pl.pallas_call(
        cells_kernel,
        out_shape=[
            jax.ShapeDtypeStruct((n, 2 * (nf + TAIL), 2 * width), jnp.int16),
            jax.ShapeDtypeStruct((n, nf + TAIL, 2 * width), jnp.int16),
        ]
        + [shape(tiles, joint // 8, 2, 8, 128)] * 2
        + [jax.ShapeDtypeStruct((joint, 2 * nt), BF16)],
        in_specs=[VM] * 4,
        out_specs=[VM] * 5,
        scratch_shapes=[
            pltpu.VMEM((nf, joint), F32),
            pltpu.VMEM((nt, joint), F32),
            pltpu.VMEM((nf, joint), F32),
            pltpu.VMEM((nt, joint), F32),
            pltpu.VMEM((nt, 128), jnp.int32),
            pltpu.VMEM((nf, 2 * nt), F32),
            pltpu.VMEM((FB * nt, vocab), F32),
            pltpu.VMEM((cells, joint + vocab), BF16),
        ],
        compiler_params=pltpu.CompilerParams(vmem_limit_bytes=40 * 1024 * 1024),
        name="joint_cells",
    )(gathered, partner, weights, per_cell)

    term_recv, ow_send = lax.optimization_barrier((swap(term_send), ow_send))
    ow_recv = swap(ow_send)
    sums = lax.dynamic_update_slice(term_keep, term_recv, (0, nf + TAIL, 0))
    summed = exchange(sums)
    payload, own = pl.pallas_call(
        pack_kernel,
        out_shape=[
            jax.ShapeDtypeStruct((joint // 4, tiles * 8 + SMALL, 128), jnp.int16),
            shape(2 * nf, 2 * width),
        ],
        in_specs=[VM] * 4,
        out_specs=[VM] * 2,
        scratch_shapes=[pltpu.VMEM((joint // 8, 2, SMALL, 2 * width), F32)],
        compiler_params=pltpu.CompilerParams(vmem_limit_bytes=16 * 1024 * 1024),
        name="pack_shares",
    )(ow_keep, ow_recv, summed, features)
    partner_own = swap(own)
    shares = lax.all_to_all(payload, ALL, 0, 0)
    own_rows = joint // 128
    enc_grad, pred_grad, enc_wgrad, pred_wgrad, out_wgrad, bias_grad = pl.pallas_call(
        last_kernel,
        out_shape=[
            shape(1, nf, width), shape(1, nt, width), shape(own_rows, joint), shape(own_rows, joint),
            shape(own_rows, vocab), shape(1, own_rows),
        ],
        in_specs=[VM] * 3,
        out_specs=[VM] * 6,
        compiler_params=pltpu.CompilerParams(vmem_limit_bytes=24 * 1024 * 1024),
        name="sum_shares",
    )(shares, own, partner_own)
    return enc_grad, pred_grad, enc_wgrad, pred_wgrad, out_wgrad, bias_grad[0]


def solution(mesh):
    in_specs = (
        P("batch", "frame", "token"),
        P("batch", "token", "frame"),
        P(),
        P(),
        P(),
        P(),
        P("batch", "frame", "token"),
        P("batch", "frame", "token"),
        P(),
        P(),
        P(None, "token"),
    )
    out_specs = (
        P("batch", "frame", "token"),
        P("batch", "token", "frame"),
        P(ALL, None),
        P(ALL, None),
        P(ALL, None),
        P(ALL),
    )
    return jax.shard_map(local, mesh=mesh, in_specs=in_specs, out_specs=out_specs, check_vma=False)
```

profile of v0, /device:TPU:1, one launch (start us, length us, event | category | flops | bytes accessed | tf_op | source)
XLA Modules:
  0.0 77.0 jit_solution(1058297609715289006)
XLA Ops:
  0.6 1.5 %collective-permute-start.1 = (bf16[64,64]{1,0:T(8,128)(2,1)}, bf16[64,64]{1,0:T(8,128)(2,1)S(1)}, u32[]{:S(2)}, u32[]{:S(2)}) collective-permute-start(bf16[64,64]{1,0:T(8,128)(2,1)} %bitcast.12), channel_id=1, source_target_pairs={{0,1},{1,0},{2,3},{3,2},{4,5},{5,4},{6,7},{7,6},{8,9},{9,8},{10,11... | collective-permute-start | bytes 24584 | tf_op jit(solution)/shard_map/ppermute | solution.py:266
  2.1 0.1 collective-permute-start
  2.2 0.7 select_bitcast_fusion
  3.0 0.2 collective-permute-done.1
  3.2 0.3 collective-permute-done
  3.6 0.8 %pad_maximum_fusion.1 = bf16[8,64,128]{2,1,0:T(8,128)(2,1)} fusion(bf16[8,64,64]{2,1,0:T(8,128)(2,1)S(1)} %broadcast_in_dim.8, bf16[8,64,64]{2,1,0:T(8,128)(2,1)S(1)} %broadcast_in_dim.7), kind=kLoop, calls=%fused_computation.1 | loop fusion | flops 262144 | bytes 262144 | tf_op jit(solution)/shard_map/concatenate | solution.py:275
  4.4 7.7 %all-to-all-start = ((bf16[8,64,128]{2,1,0:T(8,128)(2,1)}), bf16[8,64,128]{2,1,0:T(8,128)(2,1)S(1)}, u32[]{:S(2)}, u32[]{:S(2)}) async-start(bf16[8,64,128]{2,1,0:T(8,128)(2,1)} %pad_maximum_fusion.1), calls=%async_computation | async-start | bytes 262144 | tf_op jit(solution)/shard_map/all_to_all | solution.py:269
  12.1 0.0 copy-start.4
  12.1 0.0 copy-start.5
  12.1 0.0 copy-start.3
  12.1 0.0 copy-start
  12.2 0.0 copy-start.1
  12.2 0.0 copy-start.2
  12.2 1.8 %pad_maximum_fusion.weights_ref = bf16[512,2048]{1,0:T(8,128)(2,1)S(1)} fusion(bf16[512,512]{1,0:T(8,128)(2,1)} %param.14, bf16[512,512]{1,0:T(8,128)(2,1)} %param.13, bf16[512,1024]{1,0:T(8,128)(2,1)} %param.16), kind=kLoop, calls=%fused_computation | loop fusion | flops 6291456 | bytes 4194304 | tf_op jit(solution)/shard_map/concatenate | solution.py:296
  14.0 0.0 copy-done.4
  14.0 0.0 copy-done.5
  14.0 0.1 add_convert_fusion
  14.1 0.0 copy-done.3
  14.1 0.1 reshape.49
  14.1 0.0 copy-done
  14.1 0.0 copy-done.1
  14.2 0.0 copy-done.2
  14.2 0.1 select_maximum_fusion.cell_ref
  14.2 5.1 %all-to-all-done.g_ref = bf16[8,64,128]{2,1,0:T(8,128)(2,1)S(1)} async-done(((bf16[8,64,128]{2,1,0:T(8,128)(2,1)}), bf16[8,64,128]{2,1,0:T(8,128)(2,1)S(1)}, u32[]{:S(2)}, u32[]{:S(2)}) %all-to-all-start) | async-done | bytes 131104 | tf_op jit(solution)/shard_map/all_to_all | solution.py:269
  19.3 0.0 collective-permute-start.2
  19.3 1.3 %collective-permute-done.2.h_ref = bf16[8,64,128]{2,1,0:T(8,128)(2,1)S(1)} collective-permute-done((bf16[8,64,128]{2,1,0:T(8,128)(2,1)S(1)}, bf16[8,64,128]{2,1,0:T(8,128)(2,1)S(1)}, u32[]{:S(2)}, u32[]{:S(2)}) %collective-permute-start.2) | collective-permute-done | bytes 131104 | tf_op jit(solution)/shard_map/ppermute | solution.py:266
  20.6 17.6 %joint_cells.1 = (s16[8,160,128]{2,1,0:T(8,128)(2,1)S(1)}, s16[8,80,128]{2,1,0:T(8,128)(2,1)S(1)}, f32[2,64,2,8,128]{4,3,2,1,0:T(8,128)S(1)}, f32[2,64,2,8,128]{4,3,2,1,0:T(8,128)S(1)}, bf16[512,128]{1,0:T(8,128)(2,1)S(1)}) custom-call(bf16[8,64,128]{2,1,0:T(8,128)(2,1)S(1)} %all-to-all-done.g_ref, bf16[8,64,128]{2,1,0:T(8,128)(2,1)S(1)} %collective-permute-done.2.h_ref, ...), custom_call_target="tpu_custom_call" | custom-call | tf_op jit(solution)/shard_map/joint_cells/pallas_call | solution.py:300
  38.2 0.2 collective-permute-start.3
  38.5 1.2 %collective-permute-done.3 = s16[8,80,128]{2,1,0:T(8,128)(2,1)S(1)} collective-permute-done((s16[8,80,128]{2,1,0:T(8,128)(2,1)S(1)}, s16[8,80,128]{2,1,0:T(8,128)(2,1)S(1)}, u32[]{:S(2)}, u32[]{:S(2)}) %collective-permute-start.3) | collective-permute-done | bytes 163872 | tf_op jit(solution)/shard_map/ppermute | solution.py:266
  39.7 0.2 collective-permute-start.4
  39.9 12.8 %all_to_all.15.y_ref = s16[8,160,128]{2,1,0:T(8,128)(2,1)S(1)} all-to-all(s16[8,160,128]{2,1,0:T(8,128)(2,1)S(1)} %constant_dynamic-update-slice_fusion), channel_id=1, replica_groups={{0,2,4,6,8,10,12,14},{16,18,20,22,24,26,28,30},{32,34,36,38,40,42,44,46..., dimensions={0} | all-to-all | bytes 655360 | tf_op jit(solution)/shard_map/all_to_all | solution.py:269
  52.7 0.0 collective-permute-done.4.recv_ref
  52.7 2.2 %pack_shares.1 = (s16[128,24,128]{2,1,0:T(8,128)(2,1)}, f32[128,128]{1,0:T(8,128)S(1)}) custom-call(f32[2,64,2,8,128]{4,3,2,1,0:T(8,128)S(1)} %get-tuple-element.47.keep_ref, f32[2,64,2,8,128]{4,3,2,1,0:T(8,128)S(1)} %collective-permute-done.4.recv_ref, s16[8,160,128]{2,1,0:T(8,128)(2,1)S(1)} %all_to_all.15.y_ref, ...), custom_call_target="tpu_custom_call" | custom-call | tf_op jit(solution)/shard_map/pack_shares/pallas_call | solution.py:328
  54.9 4.3 %all-to-all-start.2 = ((s16[128,24,128]{2,1,0:T(8,128)(2,1)}), s16[128,24,128]{2,1,0:T(8,128)(2,1)S(1)}, u32[]{:S(2)}, u32[]{:S(2)}) async-start(s16[128,24,128]{2,1,0:T(8,128)(2,1)} %get-tuple-element.54), calls=%async_computation.2 | async-start | bytes 1572864 | tf_op jit(solution)/shard_map/all_to_all | solution.py:341
  59.2 1.1 %collective-permute-start.5 = (f32[128,128]{1,0:T(8,128)S(1)}, f32[128,128]{1,0:T(8,128)S(1)}, u32[]{:S(2)}, u32[]{:S(2)}) collective-permute-start(f32[128,128]{1,0:T(8,128)S(1)} %get-tuple-element.55.own_ref), channel_id=1, source_target_pairs={{0,1},{1,0},{2,3},{3,2},{4,5},{5,4},{6,7},{7,6},{8,9},{9,8},{10,11... | collective-permute-start | bytes 196616 | tf_op jit(solution)/shard_map/ppermute | solution.py:266
  60.3 0.9 %collective-permute-done.5.partner_ref = f32[128,128]{1,0:T(8,128)S(1)} collective-permute-done((f32[128,128]{1,0:T(8,128)S(1)}, f32[128,128]{1,0:T(8,128)S(1)}, u32[]{:S(2)}, u32[]{:S(2)}) %collective-permute-start.5) | collective-permute-done | bytes 65568 | tf_op jit(solution)/shard_map/ppermute | solution.py:266
  61.2 14.6 %all-to-all-done.2.z_ref = s16[128,24,128]{2,1,0:T(8,128)(2,1)S(1)} async-done(((s16[128,24,128]{2,1,0:T(8,128)(2,1)}), s16[128,24,128]{2,1,0:T(8,128)(2,1)S(1)}, u32[]{:S(2)}, u32[]{:S(2)}) %all-to-all-start.2) | async-done | bytes 786464 | tf_op jit(solution)/shard_map/all_to_all | solution.py:341
  75.8 1.1 %sum_shares.1 = (f32[1,64,64]{2,1,0:T(8,128)}, f32[1,64,64]{2,1,0:T(8,128)}, f32[4,512]{1,0:T(4,128)}, f32[4,512]{1,0:T(4,128)}, f32[4,1024]{1,0:T(4,128)}, /*index=5*/f32[1,4]{1,0:T(1,128)}) custom-call(s16[128,24,128]{2,1,0:T(8,128)(2,1)S(1)} %all-to-all-done.2.z_ref, f32[128,128]{1,0:T(8,128)S(1)} %get-tuple-element.55.own_ref, ...), custom_call_target="tpu_custom_call" | custom-call | tf_op jit(solution)/shard_map/sum_shares/pallas_call | solution.py:343
  (5 shorter events, 0.1 us)
Async XLA Ops:
  0.6 2.6 %collective-permute-start.1 = (bf16[64,64]{1,0:T(8,128)(2,1)}, bf16[64,64]{1,0:T(8,128)(2,1)S(1)}, u32[]{:S(2)}, u32[]{:S(2)}) collective-permute-start(bf16[64,64]{1,0:T(8,128)(2,1)} %bitcast.12), channel_id=1, source_target_pairs={{0,1},{1,0},{2,3},{3,2},{4,5},{5,4},{6,7},{7,6},{8,9},{9,8},{10,11... | collective-permute-start | bytes 24584 | tf_op jit(solution)/shard_map/ppermute | solution.py:266
  2.1 1.4 %collective-permute-start = (bf16[64,64]{1,0:T(8,128)(2,1)}, bf16[64,64]{1,0:T(8,128)(2,1)S(1)}, u32[]{:S(2)}, u32[]{:S(2)}) collective-permute-start(bf16[64,64]{1,0:T(8,128)(2,1)} %bitcast.13), channel_id=1, source_target_pairs={{0,1},{1,0},{2,3},{3,2},{4,5},{5,4},{6,7},{7,6},{8,9},{9,8},{10,11... | collective-permute-start | bytes 24584 | tf_op jit(solution)/shard_map/ppermute | solution.py:266
  4.4 14.9 %all-to-all-start = ((bf16[8,64,128]{2,1,0:T(8,128)(2,1)}), bf16[8,64,128]{2,1,0:T(8,128)(2,1)S(1)}, u32[]{:S(2)}, u32[]{:S(2)}) async-start(bf16[8,64,128]{2,1,0:T(8,128)(2,1)} %pad_maximum_fusion.1), calls=%async_computation | async-start | bytes 262144 | tf_op jit(solution)/shard_map/all_to_all | solution.py:269
  12.1 1.8 %copy-start.4 = (s32[2]{0:T(128)S(1)}, s32[2]{0:T(128)}, u32[]{:S(2)}) copy-start(s32[2]{0:T(128)} %param.20) | copy-start | bytes 28
  12.1 1.9 %copy-start.5 = (s32[2]{0:T(128)S(1)}, s32[2]{0:T(128)}, u32[]{:S(2)}) copy-start(s32[2]{0:T(128)} %param.19) | copy-start | bytes 28
  12.1 1.9 %copy-start.3 = (s32[2,64]{1,0:T(2,128)S(1)}, s32[2,64]{1,0:T(2,128)}, u32[]{:S(2)}) copy-start(s32[2,64]{1,0:T(2,128)} %param.21) | copy-start | bytes 1540
  12.1 2.0 %copy-start = (f32[1,64,64]{2,1,0:T(8,128)S(1)}, f32[1,64,64]{2,1,0:T(8,128)}, u32[]{:S(2)}) copy-start(f32[1,64,64]{2,1,0:T(8,128)} %param.18) | copy-start | bytes 49156
  12.2 2.0 %copy-start.1 = (f32[1,64,64]{2,1,0:T(8,128)S(1)}, f32[1,64,64]{2,1,0:T(8,128)}, u32[]{:S(2)}) copy-start(f32[1,64,64]{2,1,0:T(8,128)} %param.17) | copy-start | bytes 49156
  12.2 2.0 %copy-start.2 = (f32[512]{0:T(512)S(1)}, f32[512]{0:T(512)}, u32[]{:S(2)}) copy-start(f32[512]{0:T(512)} %param.15) | copy-start | bytes 6148
  19.3 1.3 %collective-permute-start.2 = (bf16[8,64,128]{2,1,0:T(8,128)(2,1)S(1)}, bf16[8,64,128]{2,1,0:T(8,128)(2,1)S(1)}, u32[]{:S(2)}, u32[]{:S(2)}) collective-permute-start(bf16[8,64,128]{2,1,0:T(8,128)(2,1)S(1)} %all-to-all-done.g_ref), channel_id=1, source_target_pairs={{0,1},{1,0},{2,3},{3,2},{4,5},{5,4},{6,7},{7,6},{8,9},{9,8},{10,11... | collective-permute-start | bytes 393224 | tf_op jit(solution)/shard_map/ppermute | solution.py:266
  38.2 1.5 %collective-permute-start.3 = (s16[8,80,128]{2,1,0:T(8,128)(2,1)S(1)}, s16[8,80,128]{2,1,0:T(8,128)(2,1)S(1)}, u32[]{:S(2)}, u32[]{:S(2)}) collective-permute-start(s16[8,80,128]{2,1,0:T(8,128)(2,1)S(1)} %get-tuple-element.48), channel_id=1, source_target_pairs={{0,1},{1,0},{2,3},{3,2},{4,5},{5,4},{6,7},{7,6},{8,9},{9,8},{10,11... | collective-permute-start | bytes 491528 | tf_op jit(solution)/shard_map/ppermute | solution.py:266
  39.7 13.0 %collective-permute-start.4 = (f32[2,64,2,8,128]{4,3,2,1,0:T(8,128)S(1)}, f32[2,64,2,8,128]{4,3,2,1,0:T(8,128)S(1)}, u32[]{:S(2)}, u32[]{:S(2)}) collective-permute-start(f32[2,64,2,8,128]{4,3,2,1,0:T(8,128)S(1)} %get-tuple-element.50), channel_id=1, source_target_pairs={{0,1},{1,0},{2,3},{3,2},{4,5},{5,4},{6,7},{7,6},{8,9},{9,8},{10,11... | collective-permute-start | bytes 3145736 | tf_op jit(solution)/shard_map/ppermute | solution.py:266
  54.9 20.9 %all-to-all-start.2 = ((s16[128,24,128]{2,1,0:T(8,128)(2,1)}), s16[128,24,128]{2,1,0:T(8,128)(2,1)S(1)}, u32[]{:S(2)}, u32[]{:S(2)}) async-start(s16[128,24,128]{2,1,0:T(8,128)(2,1)} %get-tuple-element.54), calls=%async_computation.2 | async-start | bytes 1572864 | tf_op jit(solution)/shard_map/all_to_all | solution.py:341
  59.2 2.0 %collective-permute-start.5 = (f32[128,128]{1,0:T(8,128)S(1)}, f32[128,128]{1,0:T(8,128)S(1)}, u32[]{:S(2)}, u32[]{:S(2)}) collective-permute-start(f32[128,128]{1,0:T(8,128)S(1)} %get-tuple-element.55.own_ref), channel_id=1, source_target_pairs={{0,1},{1,0},{2,3},{3,2},{4,5},{5,4},{6,7},{7,6},{8,9},{9,8},{10,11... | collective-permute-start | bytes 196616 | tf_op jit(solution)/shard_map/ppermute | solution.py:266
where the time goes:
time: 77.4 us; the launch traced here: 77 us
  waiting for transfers between devices  23.7 us (31%)
  Pallas kernels  20.9 us (27%)
  starting transfers between devices  15.1 us (20%)
  blocking collectives  12.8 us (17%)
  other arithmetic  3.44 us (4%)
    pallas_call x1, Pallas kernels, local(): pl.pallas_call(cells_kernel, out_shape=[jax.ShapeDtypeStruct((n, 2 * (nf...  17.6 us
    all_to_all x1, waiting for transfers between devices, local(): shares = lax.all_to_all(payload, ALL, 0, 0)  14.6 us
    all_to_all x1, blocking collectives, exchange(): return lax.all_to_all(x, ALL, 0, 0, axis_index_groups=groups)  12.8 us
    all_to_all x1, starting transfers between devices, exchange(): return lax.all_to_all(x, ALL, 0, 0, axis_index_groups=groups)  7.75 us
    all_to_all x1, waiting for transfers between devices, exchange(): return lax.all_to_all(x, ALL, 0, 0, axis_index_groups=groups)  5.07 us
    all_to_all x1, starting transfers between devices, local(): shares = lax.all_to_all(payload, ALL, 0, 0)  4.26 us
    ppermute x6, waiting for transfers between devices, swap(): return lax.ppermute(x, 'batch', [(0, 1), (1, 0)])  4.06 us
    ppermute x6, starting transfers between devices, swap(): return lax.ppermute(x, 'batch', [(0, 1), (1, 0)])  3.14 us
  transfers between devices with their start and end apart: 8, of which 7 were waited for; matrix products, arithmetic and copies ran while one was open for 4% of the time, Pallas kernels for 0%

commit v1 on v0

--- a/solution.py
+++ b/solution.py
@@ -165,9 +165,7 @@
             dest_ref[v, :, 1] = jnp.where(top, pltpu.roll(a, 4, 1), b)
 
 
-def pack_kernel(keep_ref, recv_ref, y_ref, feat_ref, out_ref, total_ref, small_ref):
-    tiles, chips = keep_ref.shape[:2]
-    big = tiles * 8
+def sum_kernel(y_ref, total_ref):
     span = y_ref.shape[1] // 2
     nt = span - TAIL
     for h in range(2):
@@ -176,6 +174,11 @@
             x = y_ref[s, h * span : (h + 1) * span, :].astype(jnp.int32).astype(F32)
             total = total + from_levels(x[:nt], x[nt : nt + 1])
         total_ref[h * nt : (h + 1) * nt, :] = total
+
+
+def pack_kernel(keep_ref, recv_ref, total_ref, feat_ref, out_ref, small_ref):
+    tiles, chips = keep_ref.shape[:2]
+    big = tiles * 8
     total = total_ref[...]
     width = total.shape[1] // 2
     rows_grad = total[:, width:]
@@ -325,19 +328,25 @@
     ow_recv = swap(ow_send)
     sums = lax.dynamic_update_slice(term_keep, term_recv, (0, nf + TAIL, 0))
     summed = exchange(sums)
-    payload, own = pl.pallas_call(
+    own = pl.pallas_call(
+        sum_kernel,
+        out_shape=shape(2 * nf, 2 * width),
+        in_specs=[VM],
+        out_specs=VM,
+        compiler_params=pltpu.CompilerParams(vmem_limit_bytes=16 * 1024 * 1024),
+        name="sum_rows",
+    )(summed)
+    partner_own = swap(own)
+    payload = pl.pallas_call(
         pack_kernel,
-        out_shape=[
-            jax.ShapeDtypeStruct((joint // 4, tiles * 8 + SMALL, 128), jnp.int16),
-            shape(2 * nf, 2 * width),
-        ],
+        out_shape=jax.ShapeDtypeStruct((joint // 4, tiles * 8 + SMALL, 128), jnp.int16),
         in_specs=[VM] * 4,
-        out_specs=[VM] * 2,
+        out_specs=VM,
         scratch_shapes=[pltpu.VMEM((joint // 8, 2, SMALL, 2 * width), F32)],
         compiler_params=pltpu.CompilerParams(vmem_limit_bytes=16 * 1024 * 1024),
         name="pack_shares",
-    )(ow_keep, ow_recv, summed, features)
-    partner_own = swap(own)
+    )(ow_keep, ow_recv, own, features)
+    payload, partner_own = lax.optimization_barrier((payload, partner_own))
     shares = lax.all_to_all(payload, ALL, 0, 0)
     own_rows = joint // 128
     enc_grad, pred_grad, enc_wgrad, pred_wgrad, out_wgrad, bias_grad = pl.pallas_call(

time: 77.4 us -> 76.7 us (level)
  blocking collectives: 12.8 us -> 33.8 us
  waiting for transfers between devices: 23.7 us -> 8.39 us
  starting transfers between devices: 15.1 us -> 9.79 us
  Pallas kernels: 20.9 us -> 20 us
    all_to_all x0 -> x1, blocking collectives: none -> 21 us  [local(): shares = lax.all_to_all(payload, ALL, 0, 0)]
    all_to_all x1 -> x0, waiting for transfers between devices: 14.6 us -> none  [local(): shares = lax.all_to_all(payload, ALL, 0, 0)]
    all_to_all x1 -> x0, starting transfers between devices: 4.26 us -> none  [local(): shares = lax.all_to_all(payload, ALL, 0, 0)]
    ppermute x6, starting transfers between devices: 3.14 us -> 2.04 us  [swap(): return lax.ppermute(x, 'batch', [(0, 1), (1, 0)])]
    pallas_call x1 -> x2, Pallas kernels: 2.19 us -> 1.3 us  [the longest x1 1.08 us: local(): pl.pallas_call(pack_kernel, out_shape=jax.ShapeDtypeStruct((joint // 4, t...]
  transfers between devices with their start and end apart: 8 -> 7, of which waited for: 7 -> 6; matrix products, arithmetic and copies ran while one was open for 4% -> 4% of each run, Pallas kernels for 0% -> 2%
where the time goes in v1:
time: 76.7 us; the launch traced here: 76.4 us
  blocking collectives  33.8 us (44%)
  Pallas kernels  20 us (26%)
  starting transfers between devices  9.79 us (13%)
  waiting for transfers between devices  8.39 us (11%)
  other arithmetic  3.43 us (4%)
  between operations  0.77 us (1%)
    all_to_all x1, blocking collectives, local(): shares = lax.all_to_all(payload, ALL, 0, 0)  21 us
    pallas_call x1, Pallas kernels, local(): pl.pallas_call(cells_kernel, out_shape=[jax.ShapeDtypeStruct((n, 2 * (nf...  17.6 us
    all_to_all x1, blocking collectives, exchange(): return lax.all_to_all(x, ALL, 0, 0, axis_index_groups=groups)  12.8 us
    all_to_all x1, starting transfers between devices, exchange(): return lax.all_to_all(x, ALL, 0, 0, axis_index_groups=groups)  7.75 us
    all_to_all x1, waiting for transfers between devices, exchange(): return lax.all_to_all(x, ALL, 0, 0, axis_index_groups=groups)  5.07 us
    ppermute x6, waiting for transfers between devices, swap(): return lax.ppermute(x, 'batch', [(0, 1), (1, 0)])  3.33 us
    ppermute x6, starting transfers between devices, swap(): return lax.ppermute(x, 'batch', [(0, 1), (1, 0)])  2.04 us
    concatenate x1, other arithmetic, local(): weights = jnp.concatenate([out_weight, enc_weight, pred_weight], axis=1)  1.77 us
  transfers between devices with their start and end apart: 7, of which 6 were waited for; matrix products, arithmetic and copies ran while one was open for 4% of the time, Pallas kernels for 2%

profile of v1, /device:TPU:1, one launch (start us, length us, event | category | flops | bytes accessed | tf_op | source)
XLA Modules:
  0.0 76.4 jit_solution(3832497125084075816)
XLA Ops:
  0.6 1.5 %collective-permute-start.1 = (bf16[64,64]{1,0:T(8,128)(2,1)}, bf16[64,64]{1,0:T(8,128)(2,1)S(1)}, u32[]{:S(2)}, u32[]{:S(2)}) collective-permute-start(bf16[64,64]{1,0:T(8,128)(2,1)} %bitcast.12), channel_id=1, source_target_pairs={{0,1},{1,0},{2,3},{3,2},{4,5},{5,4},{6,7},{7,6},{8,9},{9,8},{10,11... | collective-permute-start | bytes 24584 | tf_op jit(solution)/shard_map/ppermute | solution.py:269
  2.1 0.1 collective-permute-start
  2.2 0.7 select_bitcast_fusion
  3.0 0.2 collective-permute-done.1
  3.2 0.3 collective-permute-done
  3.6 0.8 %pad_maximum_fusion.1 = bf16[8,64,128]{2,1,0:T(8,128)(2,1)} fusion(bf16[8,64,64]{2,1,0:T(8,128)(2,1)S(1)} %broadcast_in_dim.8, bf16[8,64,64]{2,1,0:T(8,128)(2,1)S(1)} %broadcast_in_dim.7), kind=kLoop, calls=%fused_computation.1 | loop fusion | flops 262144 | bytes 262144 | tf_op jit(solution)/shard_map/concatenate | solution.py:278
  4.4 7.7 %all-to-all-start = ((bf16[8,64,128]{2,1,0:T(8,128)(2,1)}), bf16[8,64,128]{2,1,0:T(8,128)(2,1)S(1)}, u32[]{:S(2)}, u32[]{:S(2)}) async-start(bf16[8,64,128]{2,1,0:T(8,128)(2,1)} %pad_maximum_fusion.1), calls=%async_computation | async-start | bytes 262144 | tf_op jit(solution)/shard_map/all_to_all | solution.py:272
  12.1 0.0 copy-start.4
  12.1 0.0 copy-start.5
  12.1 0.0 copy-start.3
  12.1 0.0 copy-start
  12.1 0.0 copy-start.1
  12.2 0.0 copy-start.2
  12.2 1.8 %pad_maximum_fusion.weights_ref = bf16[512,2048]{1,0:T(8,128)(2,1)S(1)} fusion(bf16[512,512]{1,0:T(8,128)(2,1)} %param.14, bf16[512,512]{1,0:T(8,128)(2,1)} %param.13, bf16[512,1024]{1,0:T(8,128)(2,1)} %param.16), kind=kLoop, calls=%fused_computation | loop fusion | flops 6291456 | bytes 4194304 | tf_op jit(solution)/shard_map/concatenate | solution.py:299
  13.9 0.0 copy-done.4
  14.0 0.0 copy-done.5
  14.0 0.1 add_convert_fusion
  14.0 0.0 copy-done.3
  14.0 0.1 reshape.49
  14.1 0.0 copy-done
  14.1 0.0 copy-done.1
  14.1 0.0 copy-done.2
  14.1 0.1 select_maximum_fusion.cell_ref
  14.2 5.1 %all-to-all-done.g_ref = bf16[8,64,128]{2,1,0:T(8,128)(2,1)S(1)} async-done(((bf16[8,64,128]{2,1,0:T(8,128)(2,1)}), bf16[8,64,128]{2,1,0:T(8,128)(2,1)S(1)}, u32[]{:S(2)}, u32[]{:S(2)}) %all-to-all-start) | async-done | bytes 131104 | tf_op jit(solution)/shard_map/all_to_all | solution.py:272
  19.3 0.0 collective-permute-start.2
  19.3 1.3 %collective-permute-done.2.h_ref = bf16[8,64,128]{2,1,0:T(8,128)(2,1)S(1)} collective-permute-done((bf16[8,64,128]{2,1,0:T(8,128)(2,1)S(1)}, bf16[8,64,128]{2,1,0:T(8,128)(2,1)S(1)}, u32[]{:S(2)}, u32[]{:S(2)}) %collective-permute-start.2) | collective-permute-done | bytes 131104 | tf_op jit(solution)/shard_map/ppermute | solution.py:269
  20.6 17.6 %joint_cells.1 = (s16[8,160,128]{2,1,0:T(8,128)(2,1)S(1)}, s16[8,80,128]{2,1,0:T(8,128)(2,1)S(1)}, f32[2,64,2,8,128]{4,3,2,1,0:T(8,128)S(1)}, f32[2,64,2,8,128]{4,3,2,1,0:T(8,128)S(1)}, bf16[512,128]{1,0:T(8,128)(2,1)S(1)}) custom-call(bf16[8,64,128]{2,1,0:T(8,128)(2,1)S(1)} %all-to-all-done.g_ref, bf16[8,64,128]{2,1,0:T(8,128)(2,1)S(1)} %collective-permute-done.2.h_ref, ...), custom_call_target="tpu_custom_call" | custom-call | tf_op jit(solution)/shard_map/joint_cells/pallas_call | solution.py:303
  38.2 0.2 collective-permute-start.3
  38.5 1.3 %collective-permute-done.3 = s16[8,80,128]{2,1,0:T(8,128)(2,1)S(1)} collective-permute-done((s16[8,80,128]{2,1,0:T(8,128)(2,1)S(1)}, s16[8,80,128]{2,1,0:T(8,128)(2,1)S(1)}, u32[]{:S(2)}, u32[]{:S(2)}) %collective-permute-start.3) | collective-permute-done | bytes 163872 | tf_op jit(solution)/shard_map/ppermute | solution.py:269
  39.7 0.1 collective-permute-start.4
  39.9 12.8 %all_to_all.15.y_ref = s16[8,160,128]{2,1,0:T(8,128)(2,1)S(1)} all-to-all(s16[8,160,128]{2,1,0:T(8,128)(2,1)S(1)} %constant_dynamic-update-slice_fusion), channel_id=1, replica_groups={{0,2,4,6,8,10,12,14},{16,18,20,22,24,26,28,30},{32,34,36,38,40,42,44,46..., dimensions={0} | all-to-all | bytes 655360 | tf_op jit(solution)/shard_map/all_to_all | solution.py:272
  52.7 0.2 sum_rows.1.total_ref.own_ref
  52.9 0.1 collective-permute-start.5
  53.0 0.0 collective-permute-done.4.recv_ref
  53.0 1.1 %pack_shares.1 = s16[128,24,128]{2,1,0:T(8,128)(2,1)S(1)} custom-call(f32[2,64,2,8,128]{4,3,2,1,0:T(8,128)S(1)} %get-tuple-element.47.keep_ref, f32[2,64,2,8,128]{4,3,2,1,0:T(8,128)S(1)} %collective-permute-done.4.recv_ref, f32[128,128]{1,0:T(8,128)S(1)} %sum_rows.1.total_ref.own_ref, bf16[512,128]{1,0:T(8,128)(2,1)S(1)} %get-tuple-element.53.feat_ref), custom_call_target="tpu_custom_call" | custom-call | tf_op jit(solution)/shard_map/pack_shares/pallas_call | solution.py:340
  54.1 0.1 collective-permute-done.5.partner_ref
  54.3 21.0 %all_to_all.16.z_ref = s16[128,24,128]{2,1,0:T(8,128)(2,1)S(1)} all-to-all(s16[128,24,128]{2,1,0:T(8,128)(2,1)S(1)} %pack_shares.1), channel_id=1, replica_groups=mesh['frame'=8,'token'=8,'batch'=2] {'frame','token','batch'}, dimensions={0} | all-to-all | bytes 1572864 | tf_op jit(solution)/shard_map/all_to_all | solution.py:350
  75.2 1.1 %sum_shares.1 = (f32[1,64,64]{2,1,0:T(8,128)}, f32[1,64,64]{2,1,0:T(8,128)}, f32[4,512]{1,0:T(4,128)}, f32[4,512]{1,0:T(4,128)}, f32[4,1024]{1,0:T(4,128)}, /*index=5*/f32[1,4]{1,0:T(1,128)}) custom-call(s16[128,24,128]{2,1,0:T(8,128)(2,1)S(1)} %all_to_all.16.z_ref, f32[128,128]{1,0:T(8,128)S(1)} %sum_rows.1.total_ref.own_ref, ...), custom_call_target="tpu_custom_call" | custom-call | tf_op jit(solution)/shard_map/sum_shares/pallas_call | solution.py:352
  (5 shorter events, 0.1 us)
Async XLA Ops:
  0.6 2.6 %collective-permute-start.1 = (bf16[64,64]{1,0:T(8,128)(2,1)}, bf16[64,64]{1,0:T(8,128)(2,1)S(1)}, u32[]{:S(2)}, u32[]{:S(2)}) collective-permute-start(bf16[64,64]{1,0:T(8,128)(2,1)} %bitcast.12), channel_id=1, source_target_pairs={{0,1},{1,0},{2,3},{3,2},{4,5},{5,4},{6,7},{7,6},{8,9},{9,8},{10,11... | collective-permute-start | bytes 24584 | tf_op jit(solution)/shard_map/ppermute | solution.py:269
  2.1 1.4 %collective-permute-start = (bf16[64,64]{1,0:T(8,128)(2,1)}, bf16[64,64]{1,0:T(8,128)(2,1)S(1)}, u32[]{:S(2)}, u32[]{:S(2)}) collective-permute-start(bf16[64,64]{1,0:T(8,128)(2,1)} %bitcast.13), channel_id=1, source_target_pairs={{0,1},{1,0},{2,3},{3,2},{4,5},{5,4},{6,7},{7,6},{8,9},{9,8},{10,11... | collective-permute-start | bytes 24584 | tf_op jit(solution)/shard_map/ppermute | solution.py:269
  4.4 14.9 %all-to-all-start = ((bf16[8,64,128]{2,1,0:T(8,128)(2,1)}), bf16[8,64,128]{2,1,0:T(8,128)(2,1)S(1)}, u32[]{:S(2)}, u32[]{:S(2)}) async-start(bf16[8,64,128]{2,1,0:T(8,128)(2,1)} %pad_maximum_fusion.1), calls=%async_computation | async-start | bytes 262144 | tf_op jit(solution)/shard_map/all_to_all | solution.py:272
  12.1 1.8 %copy-start.4 = (s32[2]{0:T(128)S(1)}, s32[2]{0:T(128)}, u32[]{:S(2)}) copy-start(s32[2]{0:T(128)} %param.20) | copy-start | bytes 28
  12.1 1.9 %copy-start.5 = (s32[2]{0:T(128)S(1)}, s32[2]{0:T(128)}, u32[]{:S(2)}) copy-start(s32[2]{0:T(128)} %param.19) | copy-start | bytes 28
  12.1 1.9 %copy-start.3 = (s32[2,64]{1,0:T(2,128)S(1)}, s32[2,64]{1,0:T(2,128)}, u32[]{:S(2)}) copy-start(s32[2,64]{1,0:T(2,128)} %param.21) | copy-start | bytes 1540
  12.1 2.0 %copy-start = (f32[1,64,64]{2,1,0:T(8,128)S(1)}, f32[1,64,64]{2,1,0:T(8,128)}, u32[]{:S(2)}) copy-start(f32[1,64,64]{2,1,0:T(8,128)} %param.18) | copy-start | bytes 49156
  12.1 2.0 %copy-start.1 = (f32[1,64,64]{2,1,0:T(8,128)S(1)}, f32[1,64,64]{2,1,0:T(8,128)}, u32[]{:S(2)}) copy-start(f32[1,64,64]{2,1,0:T(8,128)} %param.17) | copy-start | bytes 49156
  12.2 2.0 %copy-start.2 = (f32[512]{0:T(512)S(1)}, f32[512]{0:T(512)}, u32[]{:S(2)}) copy-start(f32[512]{0:T(512)} %param.15) | copy-start | bytes 6148
  19.3 1.3 %collective-permute-start.2 = (bf16[8,64,128]{2,1,0:T(8,128)(2,1)S(1)}, bf16[8,64,128]{2,1,0:T(8,128)(2,1)S(1)}, u32[]{:S(2)}, u32[]{:S(2)}) collective-permute-start(bf16[8,64,128]{2,1,0:T(8,128)(2,1)S(1)} %all-to-all-done.g_ref), channel_id=1, source_target_pairs={{0,1},{1,0},{2,3},{3,2},{4,5},{5,4},{6,7},{7,6},{8,9},{9,8},{10,11... | collective-permute-start | bytes 393224 | tf_op jit(solution)/shard_map/ppermute | solution.py:269
  38.2 1.5 %collective-permute-start.3 = (s16[8,80,128]{2,1,0:T(8,128)(2,1)S(1)}, s16[8,80,128]{2,1,0:T(8,128)(2,1)S(1)}, u32[]{:S(2)}, u32[]{:S(2)}) collective-permute-start(s16[8,80,128]{2,1,0:T(8,128)(2,1)S(1)} %get-tuple-element.48), channel_id=1, source_target_pairs={{0,1},{1,0},{2,3},{3,2},{4,5},{5,4},{6,7},{7,6},{8,9},{9,8},{10,11... | collective-permute-start | bytes 491528 | tf_op jit(solution)/shard_map/ppermute | solution.py:269
  39.7 13.3 %collective-permute-start.4 = (f32[2,64,2,8,128]{4,3,2,1,0:T(8,128)S(1)}, f32[2,64,2,8,128]{4,3,2,1,0:T(8,128)S(1)}, u32[]{:S(2)}, u32[]{:S(2)}) collective-permute-start(f32[2,64,2,8,128]{4,3,2,1,0:T(8,128)S(1)} %get-tuple-element.50), channel_id=1, source_target_pairs={{0,1},{1,0},{2,3},{3,2},{4,5},{5,4},{6,7},{7,6},{8,9},{9,8},{10,11... | collective-permute-start | bytes 3145736 | tf_op jit(solution)/shard_map/ppermute | solution.py:269
  52.9 1.3 %collective-permute-start.5 = (f32[128,128]{1,0:T(8,128)S(1)}, f32[128,128]{1,0:T(8,128)S(1)}, u32[]{:S(2)}, u32[]{:S(2)}) collective-permute-start(f32[128,128]{1,0:T(8,128)S(1)} %sum_rows.1.total_ref.own_ref), channel_id=1, source_target_pairs={{0,1},{1,0},{2,3},{3,2},{4,5},{5,4},{6,7},{7,6},{8,9},{9,8},{10,11... | collective-permute-start | bytes 196616 | tf_op jit(solution)/shard_map/ppermute | solution.py:269

commit v2 on v1

--- a/solution.py
+++ b/solution.py
@@ -62,7 +62,7 @@
 
 
 def cells_kernel(
-    g_ref, h_ref, weights_ref, cell_ref, keep_ref, send_ref, ow_keep_ref, ow_send_ref, feat_ref,
+    g_ref, h_ref, weights_ref, cell_ref, keep_ref, send_ref, ow_keep_ref, ow_send_ref,
     encp_ref, predp_ref, rows_ref, prow_ref, tgt_col_ref, occ_ref, e_ref, stash_ref,
 ):
     nf, nt = encp_ref.shape[0], predp_ref.shape[0]
@@ -74,7 +74,6 @@
     cells = FB * nt
     first = lax.axis_index("batch") == 0
     own, other = halves(g_ref, True), halves(h_ref, False)
-    feat_ref[...] = jnp.concatenate([own.astype(F32).T, halves(g_ref, False).astype(F32).T], axis=1).astype(BF16)
     encp_ref[...] = jnp.dot(jnp.where(first, own, other), encw_ref[...], preferred_element_type=F32)
     predp = jnp.dot(jnp.where(first, other, own), predw_ref[...], preferred_element_type=F32)
     for v in range(joint // 128):
@@ -163,6 +162,11 @@
             b = acc[:, v * 256 + 128 : v * 256 + 256].reshape(chips, 8, 128)
             dest_ref[v, :, 0] = jnp.where(top, a, pltpu.roll(b, 4, 1))
             dest_ref[v, :, 1] = jnp.where(top, pltpu.roll(a, 4, 1), b)
+
+
+def features_kernel(g_ref, feat_ref):
+    parts = [halves(g_ref, side).astype(F32).T for side in (True, False)]
+    feat_ref[...] = jnp.concatenate(parts, axis=1).astype(BF16)
 
 
 def sum_kernel(y_ref, total_ref):
@@ -300,16 +304,23 @@
     gathered, weights, per_cell = lax.optimization_barrier((gathered, weights, per_cell))
     partner = swap(gathered)
     tiles = vocab // 512
-    term_keep, term_send, ow_keep, ow_send, features = pl.pallas_call(
+    features = pl.pallas_call(
+        features_kernel,
+        out_shape=jax.ShapeDtypeStruct((joint, 2 * nt), BF16),
+        in_specs=[VM],
+        out_specs=VM,
+        compiler_params=pltpu.CompilerParams(vmem_limit_bytes=16 * 1024 * 1024),
+        name="features",
+    )(gathered)
+    term_keep, term_send, ow_keep, ow_send = pl.pallas_call(
         cells_kernel,
         out_shape=[
             jax.ShapeDtypeStruct((n, 2 * (nf + TAIL), 2 * width), jnp.int16),
             jax.ShapeDtypeStruct((n, nf + TAIL, 2 * width), jnp.int16),
         ]
-        + [shape(tiles, joint // 8, 2, 8, 128)] * 2
-        + [jax.ShapeDtypeStruct((joint, 2 * nt), BF16)],
+        + [shape(tiles, joint // 8, 2, 8, 128)] * 2,
         in_specs=[VM] * 4,
-        out_specs=[VM] * 5,
+        out_specs=[VM] * 4,
         scratch_shapes=[
             pltpu.VMEM((nf, joint), F32),
             pltpu.VMEM((nt, joint), F32),

time: 76.7 us -> 76.9 us (level)
  transfers between devices with their start and end apart: 7 -> 7, of which waited for: 6 -> 5; matrix products, arithmetic and copies ran while one was open for 4% -> 4% of each run, Pallas kernels for 2% -> 2%
where the time goes in v2:
time: 76.9 us; the launch traced here: 76.5 us
  blocking collectives  33.9 us (44%)
  Pallas kernels  20.2 us (26%)
  starting transfers between devices  9.79 us (13%)
  waiting for transfers between devices  8.24 us (11%)
  other arithmetic  3.43 us (4%)
  between operations  0.78 us (1%)
    all_to_all x1, blocking collectives, local(): shares = lax.all_to_all(payload, ALL, 0, 0)  21.1 us
    pallas_call x1, Pallas kernels, local(): pl.pallas_call(cells_kernel, out_shape=[jax.ShapeDtypeStruct((n, 2 * (nf...  17.5 us
    all_to_all x1, blocking collectives, exchange(): return lax.all_to_all(x, ALL, 0, 0, axis_index_groups=groups)  12.8 us
    all_to_all x1, starting transfers between devices, exchange(): return lax.all_to_all(x, ALL, 0, 0, axis_index_groups=groups)  7.75 us
    all_to_all x1, waiting for transfers between devices, exchange(): return lax.all_to_all(x, ALL, 0, 0, axis_index_groups=groups)  5.07 us
    ppermute x6, waiting for transfers between devices, swap(): return lax.ppermute(x, 'batch', [(0, 1), (1, 0)])  3.18 us
    ppermute x6, starting transfers between devices, swap(): return lax.ppermute(x, 'batch', [(0, 1), (1, 0)])  2.05 us
    concatenate x1, other arithmetic, local(): weights = jnp.concatenate([out_weight, enc_weight, pred_weight], axis=1)  1.77 us
  transfers between devices with their start and end apart: 7, of which 5 were waited for; matrix products, arithmetic and copies ran while one was open for 4% of the time, Pallas kernels for 2%

profile of v2, /device:TPU:1, one launch (start us, length us, event | category | flops | bytes accessed | tf_op | source)
XLA Modules:
  0.0 76.5 jit_solution(9510140583810134305)
XLA Ops:
  0.6 1.5 %collective-permute-start = (bf16[64,64]{1,0:T(8,128)(2,1)}, bf16[64,64]{1,0:T(8,128)(2,1)S(1)}, u32[]{:S(2)}, u32[]{:S(2)}) collective-permute-start(bf16[64,64]{1,0:T(8,128)(2,1)} %bitcast.12), channel_id=1, source_target_pairs={{0,1},{1,0},{2,3},{3,2},{4,5},{5,4},{6,7},{7,6},{8,9},{9,8},{10,11... | collective-permute-start | bytes 24584 | tf_op jit(solution)/shard_map/ppermute | solution.py:273
  2.1 0.1 collective-permute-start.1
  2.2 0.7 select_bitcast_fusion
  3.0 0.2 collective-permute-done
  3.2 0.3 collective-permute-done.1
  3.6 0.8 %pad_maximum_fusion.1 = bf16[8,64,128]{2,1,0:T(8,128)(2,1)} fusion(bf16[8,64,64]{2,1,0:T(8,128)(2,1)S(1)} %broadcast_in_dim.8, bf16[8,64,64]{2,1,0:T(8,128)(2,1)S(1)} %broadcast_in_dim.7), kind=kLoop, calls=%fused_computation.1 | loop fusion | flops 262144 | bytes 262144 | tf_op jit(solution)/shard_map/concatenate | solution.py:282
  4.4 7.7 %all-to-all-start = ((bf16[8,64,128]{2,1,0:T(8,128)(2,1)}), bf16[8,64,128]{2,1,0:T(8,128)(2,1)S(1)}, u32[]{:S(2)}, u32[]{:S(2)}) async-start(bf16[8,64,128]{2,1,0:T(8,128)(2,1)} %pad_maximum_fusion.1), calls=%async_computation | async-start | bytes 262144 | tf_op jit(solution)/shard_map/all_to_all | solution.py:276
  12.1 0.0 copy-start.4
  12.1 0.0 copy-start.5
  12.1 0.0 copy-start.3
  12.1 0.0 copy-start
  12.1 0.0 copy-start.1
  12.2 0.0 copy-start.2
  12.2 1.8 %pad_maximum_fusion.weights_ref = bf16[512,2048]{1,0:T(8,128)(2,1)S(1)} fusion(bf16[512,512]{1,0:T(8,128)(2,1)} %param.14, bf16[512,512]{1,0:T(8,128)(2,1)} %param.13, bf16[512,1024]{1,0:T(8,128)(2,1)} %param.16), kind=kLoop, calls=%fused_computation | loop fusion | flops 6291456 | bytes 4194304 | tf_op jit(solution)/shard_map/concatenate | solution.py:303
  13.9 0.0 copy-done.4
  14.0 0.0 copy-done.5
  14.0 0.1 add_convert_fusion
  14.0 0.0 copy-done.3
  14.0 0.1 reshape.49
  14.1 0.0 copy-done
  14.1 0.0 copy-done.1
  14.1 0.0 copy-done.2
  14.1 0.1 select_maximum_fusion.cell_ref
  14.2 5.1 %all-to-all-done.g_ref = bf16[8,64,128]{2,1,0:T(8,128)(2,1)S(1)} async-done(((bf16[8,64,128]{2,1,0:T(8,128)(2,1)}), bf16[8,64,128]{2,1,0:T(8,128)(2,1)S(1)}, u32[]{:S(2)}, u32[]{:S(2)}) %all-to-all-start) | async-done | bytes 131104 | tf_op jit(solution)/shard_map/all_to_all | solution.py:276
  19.3 0.0 collective-permute-start.2
  19.3 1.3 %collective-permute-done.2.h_ref = bf16[8,64,128]{2,1,0:T(8,128)(2,1)S(1)} collective-permute-done((bf16[8,64,128]{2,1,0:T(8,128)(2,1)S(1)}, bf16[8,64,128]{2,1,0:T(8,128)(2,1)S(1)}, u32[]{:S(2)}, u32[]{:S(2)}) %collective-permute-start.2) | collective-permute-done | bytes 131104 | tf_op jit(solution)/shard_map/ppermute | solution.py:273
  20.6 17.5 %joint_cells.1 = (s16[8,160,128]{2,1,0:T(8,128)(2,1)S(1)}, s16[8,80,128]{2,1,0:T(8,128)(2,1)S(1)}, f32[2,64,2,8,128]{4,3,2,1,0:T(8,128)S(1)}, f32[2,64,2,8,128]{4,3,2,1,0:T(8,128)S(1)}) custom-call(bf16[8,64,128]{2,1,0:T(8,128)(2,1)S(1)} %all-to-all-done.g_ref, bf16[8,64,128]{2,1,0:T(8,128)(2,1)S(1)} %collective-permute-done.2.h_ref, ...), custom_call_target="tpu_custom_call" | custom-call | tf_op jit(solution)/shard_map/joint_cells/pallas_call | solution.py:315
  38.1 0.2 collective-permute-start.3
  38.4 1.3 %collective-permute-done.3 = s16[8,80,128]{2,1,0:T(8,128)(2,1)S(1)} collective-permute-done((s16[8,80,128]{2,1,0:T(8,128)(2,1)S(1)}, s16[8,80,128]{2,1,0:T(8,128)(2,1)S(1)}, u32[]{:S(2)}, u32[]{:S(2)}) %collective-permute-start.3) | collective-permute-done | bytes 163872 | tf_op jit(solution)/shard_map/ppermute | solution.py:273
  39.6 0.1 collective-permute-start.4
  39.8 12.8 %all_to_all.15.y_ref = s16[8,160,128]{2,1,0:T(8,128)(2,1)S(1)} all-to-all(s16[8,160,128]{2,1,0:T(8,128)(2,1)S(1)} %constant_dynamic-update-slice_fusion), channel_id=1, replica_groups={{0,2,4,6,8,10,12,14},{16,18,20,22,24,26,28,30},{32,34,36,38,40,42,44,46..., dimensions={0} | all-to-all | bytes 655360 | tf_op jit(solution)/shard_map/all_to_all | solution.py:276
  52.6 0.2 sum_rows.1.total_ref.own_ref
  52.8 0.1 collective-permute-start.5
  52.9 0.3 features.1.feat_ref
  53.2 0.0 collective-permute-done.4.recv_ref
  53.3 1.1 %pack_shares.1 = s16[128,24,128]{2,1,0:T(8,128)(2,1)S(1)} custom-call(f32[2,64,2,8,128]{4,3,2,1,0:T(8,128)S(1)} %get-tuple-element.46.keep_ref, f32[2,64,2,8,128]{4,3,2,1,0:T(8,128)S(1)} %collective-permute-done.4.recv_ref, f32[128,128]{1,0:T(8,128)S(1)} %sum_rows.1.total_ref.own_ref, bf16[512,128]{1,0:T(8,128)(2,1)S(1)} %features.1.feat_ref), custom_call_target="tpu_custom_call" | custom-call | tf_op jit(solution)/shard_map/pack_shares/pallas_call | solution.py:351
  54.3 0.0 collective-permute-done.5.partner_ref
  54.3 21.1 %all_to_all.16.z_ref = s16[128,24,128]{2,1,0:T(8,128)(2,1)S(1)} all-to-all(s16[128,24,128]{2,1,0:T(8,128)(2,1)S(1)} %pack_shares.1), channel_id=1, replica_groups=mesh['frame'=8,'token'=8,'batch'=2] {'frame','token','batch'}, dimensions={0} | all-to-all | bytes 1572864 | tf_op jit(solution)/shard_map/all_to_all | solution.py:361
  75.4 1.1 %sum_shares.1 = (f32[1,64,64]{2,1,0:T(8,128)}, f32[1,64,64]{2,1,0:T(8,128)}, f32[4,512]{1,0:T(4,128)}, f32[4,512]{1,0:T(4,128)}, f32[4,1024]{1,0:T(4,128)}, /*index=5*/f32[1,4]{1,0:T(1,128)}) custom-call(s16[128,24,128]{2,1,0:T(8,128)(2,1)S(1)} %all_to_all.16.z_ref, f32[128,128]{1,0:T(8,128)S(1)} %sum_rows.1.total_ref.own_ref, ...), custom_call_target="tpu_custom_call" | custom-call | tf_op jit(solution)/shard_map/sum_shares/pallas_call | solution.py:363
  (5 shorter events, 0.1 us)
Async XLA Ops:
  0.6 2.6 %collective-permute-start = (bf16[64,64]{1,0:T(8,128)(2,1)}, bf16[64,64]{1,0:T(8,128)(2,1)S(1)}, u32[]{:S(2)}, u32[]{:S(2)}) collective-permute-start(bf16[64,64]{1,0:T(8,128)(2,1)} %bitcast.12), channel_id=1, source_target_pairs={{0,1},{1,0},{2,3},{3,2},{4,5},{5,4},{6,7},{7,6},{8,9},{9,8},{10,11... | collective-permute-start | bytes 24584 | tf_op jit(solution)/shard_map/ppermute | solution.py:273
  2.1 1.4 %collective-permute-start.1 = (bf16[64,64]{1,0:T(8,128)(2,1)}, bf16[64,64]{1,0:T(8,128)(2,1)S(1)}, u32[]{:S(2)}, u32[]{:S(2)}) collective-permute-start(bf16[64,64]{1,0:T(8,128)(2,1)} %bitcast.13), channel_id=1, source_target_pairs={{0,1},{1,0},{2,3},{3,2},{4,5},{5,4},{6,7},{7,6},{8,9},{9,8},{10,11... | collective-permute-start | bytes 24584 | tf_op jit(solution)/shard_map/ppermute | solution.py:273
  4.4 14.9 %all-to-all-start = ((bf16[8,64,128]{2,1,0:T(8,128)(2,1)}), bf16[8,64,128]{2,1,0:T(8,128)(2,1)S(1)}, u32[]{:S(2)}, u32[]{:S(2)}) async-start(bf16[8,64,128]{2,1,0:T(8,128)(2,1)} %pad_maximum_fusion.1), calls=%async_computation | async-start | bytes 262144 | tf_op jit(solution)/shard_map/all_to_all | solution.py:276
  12.1 1.8 %copy-start.4 = (s32[2]{0:T(128)S(1)}, s32[2]{0:T(128)}, u32[]{:S(2)}) copy-start(s32[2]{0:T(128)} %param.20) | copy-start | bytes 28
  12.1 1.9 %copy-start.5 = (s32[2]{0:T(128)S(1)}, s32[2]{0:T(128)}, u32[]{:S(2)}) copy-start(s32[2]{0:T(128)} %param.19) | copy-start | bytes 28
  12.1 1.9 %copy-start.3 = (s32[2,64]{1,0:T(2,128)S(1)}, s32[2,64]{1,0:T(2,128)}, u32[]{:S(2)}) copy-start(s32[2,64]{1,0:T(2,128)} %param.21) | copy-start | bytes 1540
  12.1 2.0 %copy-start = (f32[1,64,64]{2,1,0:T(8,128)S(1)}, f32[1,64,64]{2,1,0:T(8,128)}, u32[]{:S(2)}) copy-start(f32[1,64,64]{2,1,0:T(8,128)} %param.18) | copy-start | bytes 49156
  12.1 2.0 %copy-start.1 = (f32[1,64,64]{2,1,0:T(8,128)S(1)}, f32[1,64,64]{2,1,0:T(8,128)}, u32[]{:S(2)}) copy-start(f32[1,64,64]{2,1,0:T(8,128)} %param.17) | copy-start | bytes 49156
  12.2 2.0 %copy-start.2 = (f32[512]{0:T(512)S(1)}, f32[512]{0:T(512)}, u32[]{:S(2)}) copy-start(f32[512]{0:T(512)} %param.15) | copy-start | bytes 6148
  19.3 1.3 %collective-permute-start.2 = (bf16[8,64,128]{2,1,0:T(8,128)(2,1)S(1)}, bf16[8,64,128]{2,1,0:T(8,128)(2,1)S(1)}, u32[]{:S(2)}, u32[]{:S(2)}) collective-permute-start(bf16[8,64,128]{2,1,0:T(8,128)(2,1)S(1)} %all-to-all-done.g_ref), channel_id=1, source_target_pairs={{0,1},{1,0},{2,3},{3,2},{4,5},{5,4},{6,7},{7,6},{8,9},{9,8},{10,11... | collective-permute-start | bytes 393224 | tf_op jit(solution)/shard_map/ppermute | solution.py:273
  38.1 1.5 %collective-permute-start.3 = (s16[8,80,128]{2,1,0:T(8,128)(2,1)S(1)}, s16[8,80,128]{2,1,0:T(8,128)(2,1)S(1)}, u32[]{:S(2)}, u32[]{:S(2)}) collective-permute-start(s16[8,80,128]{2,1,0:T(8,128)(2,1)S(1)} %get-tuple-element.47), channel_id=1, source_target_pairs={{0,1},{1,0},{2,3},{3,2},{4,5},{5,4},{6,7},{7,6},{8,9},{9,8},{10,11... | collective-permute-start | bytes 491528 | tf_op jit(solution)/shard_map/ppermute | solution.py:273
  39.6 13.6 %collective-permute-start.4 = (f32[2,64,2,8,128]{4,3,2,1,0:T(8,128)S(1)}, f32[2,64,2,8,128]{4,3,2,1,0:T(8,128)S(1)}, u32[]{:S(2)}, u32[]{:S(2)}) collective-permute-start(f32[2,64,2,8,128]{4,3,2,1,0:T(8,128)S(1)} %get-tuple-element.49), channel_id=1, source_target_pairs={{0,1},{1,0},{2,3},{3,2},{4,5},{5,4},{6,7},{7,6},{8,9},{9,8},{10,11... | collective-permute-start | bytes 3145736 | tf_op jit(solution)/shard_map/ppermute | solution.py:273
  52.8 1.5 %collective-permute-start.5 = (f32[128,128]{1,0:T(8,128)S(1)}, f32[128,128]{1,0:T(8,128)S(1)}, u32[]{:S(2)}, u32[]{:S(2)}) collective-permute-start(f32[128,128]{1,0:T(8,128)S(1)} %sum_rows.1.total_ref.own_ref), channel_id=1, source_target_pairs={{0,1},{1,0},{2,3},{3,2},{4,5},{5,4},{6,7},{7,6},{8,9},{9,8},{10,11... | collective-permute-start | bytes 196616 | tf_op jit(solution)/shard_map/ppermute | solution.py:273
